TPU v7x, 32 devices: a whole 2x2x4 slice. The times are simulated.
32 devices in a mesh: dp: 2 (over y), gx: 4 (over z), yz: 4 (over x, core).
Axes of the slice: x: 2, y: 2, z: 4, core: 2. Of those that a mesh axis runs over, the one named last changes fastest.
Arguments:
- volume: bfloat16 [2, 4, 16, 4, 2048], P('dp', None, 'gx', 'yz'), may hold values from -6 to 6
- kernel_one: bfloat16 [32, 4, 3, 3, 3], replicated, may hold values from -0.625 to 0.625
- bias_one: float32 [32], replicated, may hold values from -0.5 to 0.5
- kernel_two: bfloat16 [64, 32, 3, 3, 3], replicated, may hold values from -0.625 to 0.625
- bias_two: float32 [64], replicated, may hold values from -0.5 to 0.5
- upstream: bfloat16 [2, 64, 4, 4, 128], P('dp', None, 'gx', 'yz'), may hold values from -6 to 6
Outputs:
- features: bfloat16 [2, 64, 4, 4, 128], P('dp', None, 'gx', 'yz')
- pooled_grad: bfloat16 [2, 32, 8, 4, 512], P('dp', None, 'gx', 'yz')
- kernel_one_grad: float32 [32, 4, 3, 3, 3], replicated
- kernel_two_grad: float32 [64, 32, 3, 3, 3], replicated
All inputs are finite; a program needn't handle non-finite values.
Results may differ from a plain program's by a relative error of at most 0.01.
The roundings to bfloat16 on the way count: a program that leaves them out, or rounds other values in their place, can miss the bound.
Values may be sent and summed in bfloat16 or wider, within the bound.
A program may use at most 64 MiB of HBM per device.

v0:
```python
import functools

import jax
import jax.numpy as jnp
import numpy as np
from jax import lax
from jax.experimental import pallas as pl
from jax.experimental.pallas import tpu as pltpu
from jax.sharding import PartitionSpec as P

ZPARTS = 4
BY = 16
BZ = 128
SLOPE = 0.3
MESH = pl.DeviceIdType.MESH
F32 = jnp.float32
BF16 = jnp.bfloat16
SIDES = [(dx, dz) for dx in (-1, 0, 1) for dz in (-1, 0, 1) if (dx, dz) != (0, 0)]
PHASES = [(px, pz, py) for px in (0, 1) for pz in (0, 1) for py in (0, 1)]
TAPS = [(kx, ky, kz) for kx in range(3) for ky in range(3) for kz in range(3)]


def split_matrix():
    out = np.zeros((512, 512), np.float32)
    for fy in range(4):
        for fz in range(32):
            for rz in range(4):
                out[fy * 128 + 4 * fz + rz, rz * 128 + fy * 32 + fz] = 1
    return out


def join_matrix():
    out = np.zeros((512, 512), np.float32)
    for pz in range(2):
        for py in range(2):
            for fy in range(4):
                for fz in range(32):
                    out[pz * 256 + py * 128 + fy * 32 + fz, (2 * fy + py) * 64 + 2 * fz + pz] = 1
    return out


def tap_matrix():
    out = np.zeros((128, 8 * 256), np.float32)
    for p, (px, pz, py) in enumerate(PHASES):
        for t, (kx, ky, kz) in enumerate(TAPS):
            for c in range(4):
                row = (px + kx) * 64 + (pz + kz) * 16 + (py + ky) * 4 + c
                out[c * 27 + t, p * 256 + row] = 1
    return out


def dot(a, b):
    return jnp.dot(a, b, preferred_element_type=F32)


def dot_nt(a, b):
    return lax.dot_general(a, b, (((1,), (1,)), ((), ())), preferred_element_type=F32)


def leaky(values):
    return jnp.where(values > 0, values, SLOPE * values)


def slope_of(values):
    return jnp.where(values > 0, 1.0, SLOPE)


def kernel(
    sizes, x_ref, up_ref, k1_ref, b1_ref, k2f_ref, b2_ref, k2b_ref, split_ref, join_ref, taps_ref,
    feat_ref, pg_ref, one_ref, two_ref,
    vol, vol_x, vol_z, vol_d, mid, mid_x, mid_z, mid_d, grad, grad_x, grad_z, grad_d,
    w1, patch, pre1, im_mid, im_grad, flat_grad, part, rs, across, gathered, one_all, one_gx,
    halo_send, halo_recv, plane_send, plane_recv, gx_send, gx_recv,
):
    n_dp, n_gx, n_yz = sizes
    dp, gx, yz = (lax.axis_index("dp"), lax.axis_index("gx"), lax.axis_index("yz"))
    plane = n_dp * n_yz
    rank = dp * n_yz + yz

    def plane_peer(k):
        other = lax.rem(rank + k, plane)
        return other, (other // n_yz, gx, lax.rem(other, n_yz))

    def gx_peer(k):
        other = lax.rem(gx + k, n_gx)
        return other, (dp, other, yz)

    def exists(dx, dz):
        inside = [gx + dx >= 0, gx + dx < n_gx, yz + dz >= 0, yz + dz < n_yz]
        return functools.reduce(jnp.logical_and, inside)

    for ref in (vol_x, vol_z, vol_d, mid_x, mid_z, mid_d, grad_x, grad_z, grad_d):
        ref[...] = jnp.zeros_like(ref)

    barrier = pltpu.get_barrier_semaphore()
    for k in range(1, plane):
        pl.semaphore_signal(barrier, inc=1, device_id=plane_peer(k)[1], device_id_type=MESH)
    for k in range(1, n_gx):
        pl.semaphore_signal(barrier, inc=1, device_id=gx_peer(k)[1], device_id_type=MESH)
    corners = jnp.int32(0)
    for dx, dz in SIDES:
        if dx and dz:
            corners = corners + exists(dx, dz).astype(jnp.int32)

            @pl.when(exists(dx, dz))
            def _(dx=dx, dz=dz):
                pl.semaphore_signal(
                    barrier, inc=1, device_id=(dp, gx + dx, yz + dz), device_id_type=MESH
                )

    def piece(own, dx, dz):
        n = own.shape[0]
        i, j = (n - 1 if dx > 0 else 0, n - 1 if dz > 0 else 0)
        if dx and dz:
            return own.at[i, j]
        return own.at[i] if dx else own.at[:, j]

    def slot(bufs, dx, dz):
        i, j = (int(dx > 0), int(dz > 0))
        if dx and dz:
            return bufs[2].at[i, j]
        return bufs[0].at[i] if dx else bufs[1].at[j]

    def halo_copy(turn, own, bufs, dx, dz):
        return pltpu.make_async_remote_copy(
            src_ref=piece(own, dx, dz),
            dst_ref=slot(bufs, -dx, -dz),
            send_sem=halo_send.at[turn, SIDES.index((dx, dz))],
            recv_sem=halo_recv.at[turn, SIDES.index((-dx, -dz))],
            device_id=(dp, gx + dx, yz + dz),
            device_id_type=MESH,
        )

    def halo_start(turn, own, bufs):
        for dx, dz in SIDES:

            @pl.when(exists(dx, dz))
            def _(dx=dx, dz=dz):
                halo_copy(turn, own, bufs, dx, dz).start()

    def halo_wait(turn, own, bufs):
        for dx, dz in SIDES:

            @pl.when(exists(dx, dz))
            def _(dx=dx, dz=dz):
                halo_copy(turn, own, bufs, dx, dz).wait_send()
                halo_copy(turn, own, bufs, -dx, -dz).wait_recv()

    lanes = lax.broadcasted_iota(jnp.int32, (1, 128), 1)
    cell_z = lanes % 32

    def raw(own, bufs, x, z, more):
        n = own.shape[0]
        dx = -1 if x < 0 else int(x >= n)
        dz = -1 if z < 0 else int(z >= n)
        if not dx and not dz:
            tile = own[(x, z) + more]
        elif dx and dz:
            tile = bufs[2][(int(dx > 0), int(dz > 0)) + more]
        elif dx:
            tile = bufs[0][(int(dx > 0), z) + more]
        else:
            tile = bufs[1][(int(dz > 0), x) + more]
        return tile.astype(F32)

    def roll(tile, by):
        return pltpu.roll(tile, by % 128, 1)

    def along_z(own, bufs, x, z, more=()):
        n = own.shape[0]
        if z < 0:
            inner = roll(raw(own, bufs, x, n - 1, more), 1)
            return jnp.where(cell_z == 0, roll(raw(own, bufs, x, -1, more), -31), inner)
        if z >= n:
            inner = roll(raw(own, bufs, x, 0, more), -1)
            return jnp.where(cell_z == 31, roll(raw(own, bufs, x, n, more), 31), inner)
        return raw(own, bufs, x, z, more)

    def y_before(tile):
        return jnp.where(lanes < 32, 0.0, roll(tile, 32))

    def y_after(tile):
        return jnp.where(lanes >= 96, 0.0, roll(tile, -32))

    def fill(target, own, bufs, flip):
        rows = own.shape[3]
        for ax in range(4):
            for az in range(4):
                tiles = [along_z(own, bufs, ax - 1, az - 1, (y,)) for y in (0, 1)]
                spread = (y_before(tiles[1]), tiles[0], tiles[1], y_after(tiles[0]))
                for ay in range(4):
                    tile = spread[ay].astype(BF16)
                    for p, (px, pz, py) in enumerate(PHASES):
                        tap = (ax - px, ay - py, az - pz)
                        if tap in TAPS:
                            t = TAPS.index(tap)
                            t = 26 - t if flip else t
                            target[t * rows : (t + 1) * rows, p * 128 : (p + 1) * 128] = tile

    by_phase = dot(x_ref[...], split_ref[...])
    for x in range(4):
        for rz in range(4):
            vol[x, rz] = by_phase[x * 16 : x * 16 + 16, rz * 128 : rz * 128 + 128].astype(BF16)
    pl.semaphore_wait(barrier, plane + n_gx - 2 + corners)
    vol_bufs = (vol_x, vol_z, vol_d)
    halo_start(0, vol, vol_bufs)
    for p in range(8):
        chosen = dot(k1_ref[...], taps_ref[:, p * 256 : (p + 1) * 256])
        w1[p * 32 : (p + 1) * 32, :] = chosen.astype(BF16)
    halo_wait(0, vol, vol_bufs)

    rows16 = lax.broadcasted_iota(jnp.int32, (16, 1), 0)
    for ex in range(-1, 5):
        for ez in range(-1, 5):
            tile = along_z(vol, vol_bufs, ex, ez)
            low = pltpu.roll(tile, 4, 0)
            low = jnp.where(rows16 < 4, y_before(low), low).astype(BF16)
            high = pltpu.roll(tile, 12, 0)
            high = jnp.where(rows16 >= 12, y_after(high), high).astype(BF16)
            for q, (qx, qz, qy) in enumerate(PHASES):
                ax, az = (ex + 1 - 2 * qx, ez + 1 - 2 * qz)
                if 0 <= ax < 4 and 0 <= az < 4:
                    row = ax * 64 + az * 16
                    patch[row : row + 16, q * 128 : (q + 1) * 128] = high if qy else low
    for q, (qx, qz, qy) in enumerate(PHASES):
        pre = dot(w1[...], patch[:, q * 128 : (q + 1) * 128])
        total = jnp.zeros((32, 128), F32)
        for p in range(8):
            value = pre[p * 32 : (p + 1) * 32] + b1_ref[...]
            pre1[p * 32 : (p + 1) * 32, q * 128 : (q + 1) * 128] = value
            total = total + leaky(value)
        mid[qx, qz, qy] = (total * 0.125).astype(BF16)

    mid_bufs = (mid_x, mid_z, mid_d)
    halo_start(1, mid, mid_bufs)
    halo_wait(1, mid, mid_bufs)
    fill(im_mid, mid, mid_bufs, False)
    pre2 = dot(k2f_ref[...], im_mid[...])
    total = jnp.zeros((64, 128), F32)
    up = up_ref[...].astype(F32) * 0.125
    for p, (px, pz, py) in enumerate(PHASES):
        value = pre2[:, p * 128 : (p + 1) * 128] + b2_ref[...]
        total = total + leaky(value)
        back = (up * slope_of(value)).astype(BF16)
        grad[px, pz, py] = back
        flat_grad[:, p * 128 : (p + 1) * 128] = back
    grad_bufs = (grad_x, grad_z, grad_d)
    halo_start(2, grad, grad_bufs)
    feat_ref[...] = (total * 0.125).astype(BF16)

    two = dot_nt(flat_grad[...], im_mid[...])
    part_rows = 64 // plane
    part[:, :, 768:896] = jnp.zeros((plane, part_rows, 128), F32)
    part[:, :, 0:864] = two.reshape(plane, part_rows, 864)

    def rs_copy(k):
        other, device = plane_peer(k)
        return pltpu.make_async_remote_copy(
            src_ref=part.at[other], dst_ref=rs.at[k - 1],
            send_sem=plane_send.at[0, k - 1], recv_sem=plane_recv.at[0, k - 1],
            device_id=device, device_id_type=MESH,
        )

    def gx_copy(turn, buf, k):
        other, device = gx_peer(k)
        return pltpu.make_async_remote_copy(
            src_ref=buf.at[gx], dst_ref=buf.at[gx],
            send_sem=gx_send.at[turn, k - 1], recv_sem=gx_recv.at[turn, k - 1],
            device_id=device, device_id_type=MESH,
        )

    def plane_copy(turn, buf, k):
        other, device = plane_peer(k)
        return pltpu.make_async_remote_copy(
            src_ref=buf.at[rank], dst_ref=buf.at[rank],
            send_sem=plane_send.at[turn, k - 1], recv_sem=plane_recv.at[turn, k - 1],
            device_id=device, device_id_type=MESH,
        )

    for k in range(1, plane):
        rs_copy(k).start()

    halo_wait(2, grad, grad_bufs)
    fill(im_grad, grad, grad_bufs, True)
    back1 = dot(k2b_ref[...], im_grad[...]).astype(BF16)
    for px in range(2):
        joined = dot(back1[:, px * 512 : (px + 1) * 512], join_ref[...])
        pg_ref[:, px * 512 : (px + 1) * 512] = joined.astype(BF16)

    for k in range(1, plane):
        rs_copy(k).wait()
    mine = part[rank]
    for k in range(1, plane):
        mine = mine + rs[k - 1]
    across[gx] = mine
    for k in range(1, n_gx):
        gx_copy(0, across, k).start()

    back1 = back1.astype(F32) * 0.125
    folded = jnp.zeros((32, 128), F32)
    for p in range(8):
        grad1 = (back1 * slope_of(pre1[p * 32 : (p + 1) * 32, :])).astype(BF16)
        full = dot_nt(grad1, patch[...])
        high = full.astype(BF16)
        low = (full - high.astype(F32)).astype(BF16)
        choose = taps_ref[:, p * 256 : (p + 1) * 256]
        folded = folded + (dot_nt(high, choose) + dot_nt(low, choose))
    one_all[rank] = folded
    for k in range(1, plane):
        plane_copy(1, one_all, k).start()

    scale = 1.0 / n_dp
    for k in range(1, n_gx):
        gx_copy(0, across, k).wait()
    mine = across[0]
    for j in range(1, n_gx):
        mine = mine + across[j]
    gathered[rank] = mine * scale
    for k in range(1, plane):
        plane_copy(2, gathered, k).start()

    for k in range(1, plane):
        plane_copy(1, one_all, k).wait()
    mine = one_all[0]
    for j in range(1, plane):
        mine = mine + one_all[j]
    one_gx[gx] = mine
    for k in range(1, n_gx):
        gx_copy(1, one_gx, k).start()
    for k in range(1, plane):
        plane_copy(2, gathered, k).wait()
    two_ref[...] = gathered[...]
    for k in range(1, n_gx):
        gx_copy(1, one_gx, k).wait()
    mine = one_gx[0]
    for j in range(1, n_gx):
        mine = mine + one_gx[j]
    one_ref[...] = mine * scale


def local(sizes, volume, kernel_one, bias_one, kernel_two, bias_two, upstream):
    n_dp, n_gx, n_yz = sizes
    plane = n_dp * n_yz
    rows = 64 // plane
    x = volume.reshape(4, 4, 4, 4, 128)
    x = jnp.transpose(x, (1, 3, 0, 2, 4)).reshape(64, 512)
    k1 = jnp.pad(kernel_one.reshape(32, 108), ((0, 0), (0, 20)))
    k2 = kernel_two.reshape(64, 32, 27)
    k2f = jnp.transpose(k2, (0, 2, 1)).reshape(64, 864)
    k2b = jnp.transpose(k2, (1, 2, 0)).reshape(32, 1728)
    vmem = pl.BlockSpec(memory_space=pltpu.VMEM)

    def halos(n, more, rows):
        tile = more + (rows, 128)
        shapes = [(n, n), (2, n), (2, n), (2, 2)]
        return [pltpu.VMEM(s + tile, BF16) for s in shapes]

    feat, pg, one, two = pl.pallas_call(
        functools.partial(kernel, sizes),
        out_shape=(
            jax.ShapeDtypeStruct((64, 128), BF16),
            jax.ShapeDtypeStruct((32, 1024), BF16),
            jax.ShapeDtypeStruct((32, 128), F32),
            jax.ShapeDtypeStruct((plane, rows, 896), F32),
        ),
        in_specs=[vmem] * 10,
        out_specs=(vmem,) * 4,
        scratch_shapes=[
            *halos(4, (), 16),
            *halos(2, (2,), 32),
            *halos(2, (2,), 64),
            pltpu.VMEM((256, 256), BF16),
            pltpu.VMEM((256, 1024), BF16),
            pltpu.VMEM((256, 1024), F32),
            pltpu.VMEM((864, 1024), BF16),
            pltpu.VMEM((1728, 1024), BF16),
            pltpu.VMEM((64, 1024), BF16),
            pltpu.VMEM((plane, rows, 896), F32),
            pltpu.VMEM((plane - 1, rows, 896), F32),
            pltpu.VMEM((n_gx, rows, 896), F32),
            pltpu.VMEM((plane, rows, 896), F32),
            pltpu.VMEM((plane, 32, 128), F32),
            pltpu.VMEM((n_gx, 32, 128), F32),
            pltpu.SemaphoreType.DMA((3, 8)),
            pltpu.SemaphoreType.DMA((3, 8)),
            pltpu.SemaphoreType.DMA((3, plane - 1)),
            pltpu.SemaphoreType.DMA((3, plane - 1)),
            pltpu.SemaphoreType.DMA((2, n_gx - 1)),
            pltpu.SemaphoreType.DMA((2, n_gx - 1)),
        ],
        compiler_params=pltpu.CompilerParams(
            collective_id=0, has_side_effects=True, vmem_limit_bytes=48 * 2**20
        ),
        cost_estimate=pl.CostEstimate(
            flops=900_000_000, bytes_accessed=3_000_000, transcendentals=0
        ),
    )(
        x,
        upstream.reshape(64, 128),
        k1,
        jnp.broadcast_to(bias_one[:, None], (32, 128)),
        k2f,
        jnp.broadcast_to(bias_two[:, None], (64, 128)),
        k2b,
        jnp.asarray(split_matrix(), BF16),
        jnp.asarray(join_matrix(), BF16),
        jnp.asarray(tap_matrix(), BF16),
    )
    two = two.reshape(64, 896)[:, :864].reshape(64, 27, 32)
    two = jnp.transpose(two, (0, 2, 1)).reshape(64, 32, 3, 3, 3)
    return (
        feat.reshape(1, 64, 1, 1, 128),
        pg.reshape(1, 32, 2, 1, 512),
        one[:, :108].reshape(32, 4, 3, 3, 3),
        two,
    )


def wide_with_halo(shard, sides, width):
    for axis, dim in sides:
        size, length = (lax.axis_size(axis), shard.shape[dim])
        up = [(i, (i + 1) % size) for i in range(size - 1)]
        down = [(j, i) for i, j in up]
        last = lax.slice_in_dim(shard, length - width, length, axis=dim)
        leading = lax.slice_in_dim(shard, 0, width, axis=dim)
        before = lax.ppermute(last, axis, up)
        after = lax.ppermute(leading, axis, down)
        shard = jnp.concatenate([before, shard, after], axis=dim)
    return shard


def wide_passed_along(value, axis, steps):
    count = lax.axis_size(axis)
    leading, last = (max(0, -steps), min(count, count - steps))
    return lax.ppermute(value, axis, [(source, source + steps) for source in range(leading, last)])


def wide_correlate(padded, kernel):
    return lax.conv_general_dilated(
        padded,
        kernel,
        (1, 1, 1),
        "VALID",
        dimension_numbers=("NCDHW", "OIDHW", "NCDHW"),
        preferred_element_type=jnp.float32,
    )


def wide_kernel_grad(padded, grads):
    summed = lax.conv_general_dilated(
        padded,
        grads,
        (1, 1, 1),
        "VALID",
        dimension_numbers=("CNDHW", "IODHW", "NCDHW"),
        preferred_element_type=jnp.float32,
    )
    return jnp.transpose(summed, (1, 0, 2, 3, 4))


def wide_average_pool(field):
    extent = field.shape
    shaped = field.reshape(
        extent[0], extent[1], extent[2] // 2, 2, extent[3] // 2, 2, extent[4] // 2, 2
    )
    return jnp.mean(shaped, axis=(3, 5, 7))


def wide_spread_back(field):
    extent = field.shape
    wide = jnp.broadcast_to(
        field[:, :, :, None, :, None, :, None],
        (extent[0], extent[1], extent[2], 2, extent[3], 2, extent[4], 2),
    )
    return wide.reshape(extent[0], extent[1], extent[2] * 2, extent[3] * 2, extent[4] * 2)


def wide_leaky(values):
    return jnp.where(values > 0, values, SLOPE * values)


def wide_slope_of(values):
    return jnp.where(values > 0, 1.0, SLOPE).astype(values.dtype)


def wide_unfold(blocks, block_y, block_z):
    extent = blocks.shape
    return blocks[:, :, :, 0].reshape(extent[0], extent[1], extent[2], block_y, block_z)


def wide_refold(field):
    extent = field.shape
    return field.reshape(extent[0], extent[1], extent[2], 1, extent[3] * extent[4])


def wide_extend(field):
    z_index = lax.axis_index("yz") % ZPARTS
    extended = wide_with_halo(field, (("gx", 2),), 1)
    incoming = []
    for offset, boundary in ((ZPARTS, extended[:, :, :, -1:]), (-ZPARTS, extended[:, :, :, :1])):
        incoming.append(wide_passed_along(boundary, "yz", offset))
    extended = jnp.concatenate([incoming[0], extended, incoming[1]], axis=3)
    arrived = []
    for offset, boundary, keeper in (
        (1, extended[:, :, :, :, -1:], z_index > 0),
        (-1, extended[:, :, :, :, :1], z_index < ZPARTS - 1),
    ):
        moved = wide_passed_along(boundary, "yz", offset)
        arrived.append(jnp.where(keeper, moved, jnp.zeros_like(moved)))
    return jnp.concatenate([arrived[0], extended, arrived[1]], axis=4)


def wide_local(volume, kernel_one, bias_one, kernel_two, bias_two, upstream):
    field = wide_unfold(volume, BY, BZ)
    padded_in = wide_extend(field)
    first_pre = wide_correlate(padded_in, kernel_one) + bias_one[None, :, None, None, None]
    pooled_one = wide_average_pool(wide_leaky(first_pre)).astype(jnp.bfloat16)
    padded_mid = wide_extend(pooled_one)
    second_pre = wide_correlate(padded_mid, kernel_two) + bias_two[None, :, None, None, None]
    features = wide_average_pool(wide_leaky(second_pre)).astype(jnp.bfloat16)
    cotangent = wide_unfold(upstream, BY // 4, BZ // 4).astype(jnp.float32)
    second_grad = (wide_spread_back(cotangent) * 0.125 * wide_slope_of(second_pre)).astype(jnp.bfloat16)
    two_grad = wide_kernel_grad(padded_mid, second_grad)
    replicas = lax.axis_size("dp") * volume.shape[0]
    padded_grad = wide_extend(second_grad)
    flipped = jnp.transpose(jnp.flip(kernel_two, (2, 3, 4)), (1, 0, 2, 3, 4))
    pooled_grad = wide_correlate(padded_grad, flipped).astype(jnp.bfloat16)
    first_grad = (
        wide_spread_back(pooled_grad.astype(jnp.float32)) * 0.125 * wide_slope_of(first_pre)
    ).astype(jnp.bfloat16)
    one_grad = wide_kernel_grad(padded_in, first_grad)
    one_grad, two_grad = lax.psum((one_grad, two_grad), ("dp", "gx", "yz"))
    return (wide_refold(features), wide_refold(pooled_grad), one_grad / replicas, two_grad / replicas)


def solution(mesh):
    sizes = tuple(mesh.shape[name] for name in ("dp", "gx", "yz"))
    one_row = sizes[2] == ZPARTS and 64 % (8 * sizes[0] * sizes[2]) == 0
    return jax.shard_map(
        functools.partial(local, sizes) if one_row else wide_local,
        mesh=mesh,
        in_specs=(
            P("dp", None, "gx", "yz", None),
            P(),
            P(),
            P(),
            P(),
            P("dp", None, "gx", "yz", None),
        ),
        out_specs=(P("dp", None, "gx", "yz", None), P("dp", None, "gx", "yz", None), P(), P()),
        check_vma=False,
    )
```

profile of v0, /device:TPU:0, one launch (start us, length us, event | category | flops | bytes accessed | tf_op | source)
XLA Modules:
  0.0 38.7 jit_solution(6831577632597951700)
XLA Ops:
  0.6 0.0 copy-start.3
  0.6 1.1 %copy.33 = bf16[64,32,27]{0,2,1:T(8,128)(2,1)S(1)} copy(bf16[64,32,27]{0,1,2:T(8,128)(2,1)} %bitcast.37) | data formatting | bytes 221184 | tf_op jit(solution)/shard_map/reshape | solution.py:348
  1.7 0.0 copy-start.4
  1.7 0.0 copy-start.5
  1.8 0.0 copy-start.2
  1.8 0.2 reshape.55.k2b_ref
  2.0 0.0 copy-start.1
  2.0 0.9 %reshape.49 = bf16[4,4,4,4,128]{4,3,2,1,0:T(4,128)(2,1)S(1)} reshape(bf16[1,4,4,1,2048]{4,2,3,1,0:T(4,128)(2,1)} %param.9) | data formatting | bytes 131072 | tf_op jit(solution)/shard_map/reshape | solution.py:345
  3.0 0.0 copy-done.4
  3.0 0.1 copy.24.k2f_ref
  3.2 0.8 %copy.21 = bf16[32,4,3,3,3]{0,4,3,2,1:T(4,128)(2,1)S(1)} copy(bf16[32,4,3,3,3]{0,1,4,3,2:T(4,128)(2,1)} %param.10) | data formatting | bytes 13824 | tf_op args[1]
  4.0 0.1 copy.22
  4.1 0.0 copy-done.5
  4.1 0.0 copy-start.6
  4.1 0.1 broadcast_in_dim.5.b2_ref
  4.2 0.6 %copy-done.6 = f32[32]{0:T(128)S(1)} copy-done((f32[32]{0:T(128)S(1)}, f32[32]{0:T(128)}, u32[]{:S(2)}) %copy-start.6) | copy-done | bytes 152
  4.7 0.0 copy-start
  4.7 0.1 broadcast_in_dim.4.b1_ref
  4.8 0.0 copy-done.3
  4.8 0.0 copy-done.2
  4.8 0.0 copy-done.1
  4.8 0.6 %copy-done = bf16[1,64,1,1,128]{4,1,3,2,0:T(8,128)(2,1)S(1)} copy-done((bf16[1,64,1,1,128]{4,1,3,2,0:T(8,128)(2,1)S(1)}, bf16[1,64,1,1,128]{4,1,3,2,0:T(8,128)(2,1)}, u32[]{:S(2)}) %copy-start) | copy-done | bytes 16408
  5.5 30.3 %shard_map.120 = (bf16[64,128]{1,0:T(8,128)(2,1)S(1)}, bf16[32,1024]{1,0:T(8,128)(2,1)S(1)}, f32[32,128]{1,0:T(8,128)S(1)}, f32[8,8,896]{2,1,0:T(8,128)S(1)}) custom-call(bf16[64,512]{1,0:T(8,128)(2,1)S(1)} %bitcast.32, bf16[64,128]{1,0:T(8,128)(2,1)S(1)} %bitcast.35, bf16[32,128]{1,0:T(8,128)(2,1)S(1)} %pad.4.k1_ref, f32[32,128]{1,0:T(8,128)S(1)} %broadcast_in_dim.4.b1_ref, ...), custom_call_target="tpu_custom_call" | custom-call | flops 900000000 | bytes 3000000 | tf_op jit(solution)/shard_map/pallas_call | solution.py:358
  35.7 1.0 %copy.29 = f32[64,864]{0,1:T(8,128)} copy(f32[64,864]{1,0:T(8,128)S(1)} %bitcast.31) | data formatting | bytes 442368
  36.7 0.1 copy.25
  36.8 0.6 %copy.28 = f32[32,4,3,3,3]{0,1,4,3,2:T(4,128)} copy(f32[32,4,3,3,3]{0,4,3,2,1:T(4,128)S(1)} %reshape.58) | data formatting | bytes 27648
  37.5 0.7 %reshape.57 = bf16[1,32,2,1,512]{4,2,1,3,0:T(2,128)(2,1)} reshape(bf16[32,1024]{1,0:T(8,128)(2,1)S(1)} %get-tuple-element.9) | data formatting | bytes 131072 | tf_op jit(solution)/shard_map/reshape | solution.py:413
  38.1 0.6 %copy.36 = bf16[1,64,1,1,128]{4,1,3,2,0:T(8,128)(2,1)} copy(bf16[1,64,1,1,128]{4,1,3,2,0:T(8,128)(2,1)S(1)} %bitcast.33) | data formatting | bytes 32768
  (5 shorter events, 0.1 us)
Async XLA Ops:
  0.6 4.2 %copy-start.3 = (bf16[512,512]{1,0:T(8,128)(2,1)S(1)}, bf16[512,512]{1,0:T(8,128)(2,1)}, u32[]{:S(2)}) copy-start(bf16[512,512]{1,0:T(8,128)(2,1)} %constant.9.clone.split_ref) | copy-start | bytes 1572868
  1.7 1.3 %copy-start.4 = (bf16[64,32,3,3,3]{0,1,4,3,2:T(8,128)(2,1)S(1)}, bf16[64,32,3,3,3]{0,1,4,3,2:T(8,128)(2,1)}, u32[]{:S(2)}) copy-start(bf16[64,32,3,3,3]{0,1,4,3,2:T(8,128)(2,1)} %param.12) | copy-start | bytes 331780
  1.7 2.3 %copy-start.5 = (f32[64]{0:T(128)S(1)}, f32[64]{0:T(128)}, u32[]{:S(2)}) copy-start(f32[64]{0:T(128)} %param.13) | copy-start | bytes 772
  1.8 3.1 %copy-start.2 = (bf16[128,2048]{1,0:T(8,128)(2,1)S(1)}, bf16[128,2048]{1,0:T(8,128)(2,1)}, u32[]{:S(2)}) copy-start(bf16[128,2048]{1,0:T(8,128)(2,1)} %constant.11.clone.taps_ref) | copy-start | bytes 1572868
  2.0 2.8 %copy-start.1 = (bf16[512,512]{1,0:T(8,128)(2,1)S(1)}, bf16[512,512]{1,0:T(8,128)(2,1)}, u32[]{:S(2)}) copy-start(bf16[512,512]{1,0:T(8,128)(2,1)} %constant.10.clone.join_ref) | copy-start | bytes 1572868
  4.1 0.7 %copy-start.6 = (f32[32]{0:T(128)S(1)}, f32[32]{0:T(128)}, u32[]{:S(2)}) copy-start(f32[32]{0:T(128)} %param.11) | copy-start | bytes 388
  4.7 0.7 %copy-start = (bf16[1,64,1,1,128]{4,1,3,2,0:T(8,128)(2,1)S(1)}, bf16[1,64,1,1,128]{4,1,3,2,0:T(8,128)(2,1)}, u32[]{:S(2)}) copy-start(bf16[1,64,1,1,128]{4,1,3,2,0:T(8,128)(2,1)} %param.14) | copy-start | bytes 49156
where the time goes:
time: 39 us; the launch traced here: 38.7 us
  Pallas kernels  30.3 us (78%)
  local copies, waits for them, and re-layouts  7.72 us (20%)
  between operations  0.76 us (2%)
    pallas_call x1, Pallas kernels, local(): pl.pallas_call(functools.partial(kernel, sizes), out_shape=(jax.ShapeDtyp...  30.3 us
    unnamed x19, local copies, waits for them, and re-layouts  4.23 us
    reshape x1, local copies, waits for them, and re-layouts, local(): k2 = kernel_two.reshape(64, 32, 27)  1.09 us
    reshape x2, local copies, waits for them, and re-layouts, local(): x = volume.reshape(4, 4, 4, 4, 128)  0.97 us

commit v1 on v0

--- a/solution.py
+++ b/solution.py
@@ -2,7 +2,6 @@
 
 import jax
 import jax.numpy as jnp
-import numpy as np
 from jax import lax
 from jax.experimental import pallas as pl
 from jax.experimental.pallas import tpu as pltpu
@@ -20,33 +19,34 @@
 TAPS = [(kx, ky, kz) for kx in range(3) for ky in range(3) for kz in range(3)]
 
 
-def split_matrix():
-    out = np.zeros((512, 512), np.float32)
-    for fy in range(4):
-        for fz in range(32):
-            for rz in range(4):
-                out[fy * 128 + 4 * fz + rz, rz * 128 + fy * 32 + fz] = 1
-    return out
-
-
-def join_matrix():
-    out = np.zeros((512, 512), np.float32)
-    for pz in range(2):
-        for py in range(2):
-            for fy in range(4):
-                for fz in range(32):
-                    out[pz * 256 + py * 128 + fy * 32 + fz, (2 * fy + py) * 64 + 2 * fz + pz] = 1
-    return out
-
-
-def tap_matrix():
-    out = np.zeros((128, 8 * 256), np.float32)
-    for p, (px, pz, py) in enumerate(PHASES):
-        for t, (kx, ky, kz) in enumerate(TAPS):
-            for c in range(4):
-                row = (px + kx) * 64 + (pz + kz) * 16 + (py + ky) * 4 + c
-                out[c * 27 + t, p * 256 + row] = 1
-    return out
+def indices(size, dim):
+    shape = (1, size) if dim else (size, 1)
+    return lax.broadcasted_iota(jnp.int32, shape, dim)
+
+
+def one_hot(source, rows):
+    wide = (rows, source.shape[1])
+    row = lax.broadcasted_iota(jnp.int32, wide, 0)
+    return jnp.where(row == source, 1.0, 0.0).astype(BF16)
+
+
+def split_source():
+    col = indices(512, 1)
+    return (col % 128) // 32 * 128 + 4 * (col % 32) + col // 128
+
+
+def join_source():
+    col = indices(512, 1)
+    return col % 2 * 256 + col // 64 % 2 * 128 + col // 128 * 32 + col % 64 // 2
+
+
+def tap_source(dim):
+    at = indices(2048, dim)
+    kx = at // 64 % 4 - at // 1024
+    kz = at // 16 % 4 - at // 512 % 2
+    ky = at // 4 % 4 - at // 256 % 2
+    inside = (kx >= 0) & (kx < 3) & (ky >= 0) & (ky < 3) & (kz >= 0) & (kz < 3)
+    return jnp.where(inside, ((kx * 3 + ky) * 3 + kz) * 4 + at % 4, -1)
 
 
 def dot(a, b):
@@ -66,10 +66,11 @@
 
 
 def kernel(
-    sizes, x_ref, up_ref, k1_ref, b1_ref, k2f_ref, b2_ref, k2b_ref, split_ref, join_ref, taps_ref,
+    sizes, v_ref, up_ref, k1_ref, b1_ref, k2_ref, b2_ref,
     feat_ref, pg_ref, one_ref, two_ref,
     vol, vol_x, vol_z, vol_d, mid, mid_x, mid_z, mid_d, grad, grad_x, grad_z, grad_d,
     w1, patch, pre1, im_mid, im_grad, flat_grad, part, rs, across, gathered, one_all, one_gx,
+    cells, k1, k2f, k2b, split, join, taps, taps_t, grads1,
     halo_send, halo_recv, plane_send, plane_recv, gx_send, gx_recv,
 ):
     n_dp, n_gx, n_yz = sizes
@@ -88,9 +89,6 @@
     def exists(dx, dz):
         inside = [gx + dx >= 0, gx + dx < n_gx, yz + dz >= 0, yz + dz < n_yz]
         return functools.reduce(jnp.logical_and, inside)
-
-    for ref in (vol_x, vol_z, vol_d, mid_x, mid_z, mid_d, grad_x, grad_z, grad_d):
-        ref[...] = jnp.zeros_like(ref)
 
     barrier = pltpu.get_barrier_semaphore()
     for k in range(1, plane):
@@ -120,6 +118,15 @@
         if dx and dz:
             return bufs[2].at[i, j]
         return bufs[0].at[i] if dx else bufs[1].at[j]
+
+    sets = ((vol_x, vol_z, vol_d), (mid_x, mid_z, mid_d), (grad_x, grad_z, grad_d))
+    for dx, dz in SIDES:
+
+        @pl.when(jnp.logical_not(exists(dx, dz)))
+        def _(dx=dx, dz=dz):
+            for bufs in sets:
+                missing = slot(bufs, dx, dz)
+                missing[...] = jnp.zeros_like(missing)
 
     def halo_copy(turn, own, bufs, dx, dz):
         return pltpu.make_async_remote_copy(
@@ -161,20 +168,20 @@
             tile = bufs[0][(int(dx > 0), z) + more]
         else:
             tile = bufs[1][(int(dz > 0), x) + more]
-        return tile.astype(F32)
+        return tile
 
     def roll(tile, by):
         return pltpu.roll(tile, by % 128, 1)
 
     def along_z(own, bufs, x, z, more=()):
         n = own.shape[0]
+        if 0 <= z < n:
+            return raw(own, bufs, x, z, more)
+        near = raw(own, bufs, x, n - 1 if z < 0 else 0, more).astype(F32)
+        far = raw(own, bufs, x, z, more).astype(F32)
         if z < 0:
-            inner = roll(raw(own, bufs, x, n - 1, more), 1)
-            return jnp.where(cell_z == 0, roll(raw(own, bufs, x, -1, more), -31), inner)
-        if z >= n:
-            inner = roll(raw(own, bufs, x, 0, more), -1)
-            return jnp.where(cell_z == 31, roll(raw(own, bufs, x, n, more), 31), inner)
-        return raw(own, bufs, x, z, more)
+            return jnp.where(cell_z == 0, roll(far, -31), roll(near, 1))
+        return jnp.where(cell_z == 31, roll(far, 31), roll(near, -1))
 
     def y_before(tile):
         return jnp.where(lanes < 32, 0.0, roll(tile, 32))
@@ -182,37 +189,35 @@
     def y_after(tile):
         return jnp.where(lanes >= 96, 0.0, roll(tile, -32))
 
-    def fill(target, own, bufs, flip):
+    def places(first, end, inner):
+        return [
+            (x, z)
+            for x in range(first, end)
+            for z in range(first, end)
+            if inner == (first < x < end - 1 and first < z < end - 1)
+        ]
+
+    def fill(target, own, bufs, flip, inner):
         rows = own.shape[3]
-        for ax in range(4):
-            for az in range(4):
-                tiles = [along_z(own, bufs, ax - 1, az - 1, (y,)) for y in (0, 1)]
-                spread = (y_before(tiles[1]), tiles[0], tiles[1], y_after(tiles[0]))
-                for ay in range(4):
-                    tile = spread[ay].astype(BF16)
-                    for p, (px, pz, py) in enumerate(PHASES):
-                        tap = (ax - px, ay - py, az - pz)
-                        if tap in TAPS:
-                            t = TAPS.index(tap)
-                            t = 26 - t if flip else t
-                            target[t * rows : (t + 1) * rows, p * 128 : (p + 1) * 128] = tile
-
-    by_phase = dot(x_ref[...], split_ref[...])
-    for x in range(4):
-        for rz in range(4):
-            vol[x, rz] = by_phase[x * 16 : x * 16 + 16, rz * 128 : rz * 128 + 128].astype(BF16)
-    pl.semaphore_wait(barrier, plane + n_gx - 2 + corners)
-    vol_bufs = (vol_x, vol_z, vol_d)
-    halo_start(0, vol, vol_bufs)
-    for p in range(8):
-        chosen = dot(k1_ref[...], taps_ref[:, p * 256 : (p + 1) * 256])
-        w1[p * 32 : (p + 1) * 32, :] = chosen.astype(BF16)
-    halo_wait(0, vol, vol_bufs)
+        for x, z in places(-1, 3, inner):
+            ax, az = (x + 1, z + 1)
+            tiles = [along_z(own, bufs, x, z, (y,)) for y in (0, 1)]
+            after = y_after(tiles[0].astype(F32))
+            before = y_before(tiles[1].astype(F32))
+            for ay, tile in enumerate((before, tiles[0], tiles[1], after)):
+                tile = tile.astype(BF16)
+                for p, (px, pz, py) in enumerate(PHASES):
+                    tap = (ax - px, ay - py, az - pz)
+                    if tap in TAPS:
+                        t = TAPS.index(tap)
+                        t = 26 - t if flip else t
+                        target[t * rows : (t + 1) * rows, p * 128 : (p + 1) * 128] = tile
 
     rows16 = lax.broadcasted_iota(jnp.int32, (16, 1), 0)
-    for ex in range(-1, 5):
-        for ez in range(-1, 5):
-            tile = along_z(vol, vol_bufs, ex, ez)
+
+    def fill_patch(inner):
+        for ex, ez in places(-1, 5, inner):
+            tile = along_z(vol, sets[0], ex, ez).astype(F32)
             low = pltpu.roll(tile, 4, 0)
             low = jnp.where(rows16 < 4, y_before(low), low).astype(BF16)
             high = pltpu.roll(tile, 12, 0)
@@ -222,29 +227,79 @@
                 if 0 <= ax < 4 and 0 <= az < 4:
                     row = ax * 64 + az * 16
                     patch[row : row + 16, q * 128 : (q + 1) * 128] = high if qy else low
-    for q, (qx, qz, qy) in enumerate(PHASES):
-        pre = dot(w1[...], patch[:, q * 128 : (q + 1) * 128])
-        total = jnp.zeros((32, 128), F32)
-        for p in range(8):
-            value = pre[p * 32 : (p + 1) * 32] + b1_ref[...]
-            pre1[p * 32 : (p + 1) * 32, q * 128 : (q + 1) * 128] = value
-            total = total + leaky(value)
-        mid[qx, qz, qy] = (total * 0.125).astype(BF16)
-
-    mid_bufs = (mid_x, mid_z, mid_d)
+
+    split[...] = one_hot(split_source(), 512)
+    for c in range(4):
+        values = v_ref[c].astype(F32)
+        for y in range(16):
+            fy, ry = (y // 4, y % 4)
+            row = ry * 16 + c * 4
+            cells[row : row + 4, fy * 128 : (fy + 1) * 128] = values[:, y * 128 : (y + 1) * 128]
+    by_phase = dot(cells[...].astype(BF16), split[...]).astype(BF16)
+    at = indices(64, 1)
+    order = one_hot(at % 4 * 16 + at // 4, 64)
+    by_phase = dot(order, by_phase).astype(BF16)
+    for x in range(4):
+        for rz in range(4):
+            vol[x, rz] = by_phase[x * 16 : x * 16 + 16, rz * 128 : rz * 128 + 128]
+    pl.semaphore_wait(barrier, plane + n_gx - 2 + corners)
+    vol_bufs = sets[0]
+    halo_start(0, vol, vol_bufs)
+
+    fill_patch(True)
+    k1[...] = jnp.zeros_like(k1)
+    for t in range(27):
+        k1[t * 4 : t * 4 + 4, 0:32] = k1_ref[t].astype(F32)
+    taps[...] = one_hot(tap_source(1), 128)
+    flat_k1 = k1[...].T[0:32].astype(BF16)
+    for p in range(8):
+        chosen = dot(flat_k1, taps[:, p * 256 : (p + 1) * 256])
+        w1[p * 32 : (p + 1) * 32, :] = chosen.astype(BF16)
+    bias1 = jnp.broadcast_to(b1_ref[...], (128, 32)).T
+    bias2 = jnp.broadcast_to(b2_ref[...], (128, 64)).T
+    for j in range(7):
+        rows = k2_ref[j * 128 : min(j * 128 + 128, 864), :].astype(F32)
+        if j == 6:
+            rows = jnp.concatenate([rows, jnp.zeros((32, 64), F32)], axis=0)
+        k2f[:, j * 128 : (j + 1) * 128] = rows.T.astype(BF16)
+    halo_wait(0, vol, vol_bufs)
+
+    fill_patch(False)
+    for qx in range(2):
+        for qz in range(2):
+            q = qx * 4 + qz * 2
+            pre = dot(w1[...], patch[:, q * 128 : (q + 2) * 128])
+            total = jnp.zeros((32, 256), F32)
+            for p in range(8):
+                value = pre[p * 32 : (p + 1) * 32] + jnp.concatenate([bias1, bias1], axis=1)
+                pre1[p * 32 : (p + 1) * 32, q * 128 : (q + 2) * 128] = value
+                total = total + leaky(value)
+            for qy in range(2):
+                own = total[:, qy * 128 : (qy + 1) * 128]
+                mid[qx, qz, qy] = (own * 0.125).astype(BF16)
+
+    mid_bufs = sets[1]
     halo_start(1, mid, mid_bufs)
+    fill(im_mid, mid, mid_bufs, False, True)
+    for t in range(0, 26, 2):
+        pair = [k2_ref[u * 32 : (u + 1) * 32, :].astype(F32) for u in (t, t + 1)]
+        k2b[:, t * 64 : (t + 2) * 64] = jnp.concatenate(pair, axis=1).astype(BF16)
+    k2b[:, 1664:1728] = k2_ref[832:864, :]
+    join[...] = one_hot(join_source(), 512)
+    hot = lax.broadcasted_iota(jnp.int32, (2048, 128), 1) == tap_source(0)
+    taps_t[...] = jnp.where(hot, 1.0, 0.0).astype(BF16)
     halo_wait(1, mid, mid_bufs)
-    fill(im_mid, mid, mid_bufs, False)
-    pre2 = dot(k2f_ref[...], im_mid[...])
+    fill(im_mid, mid, mid_bufs, False, False)
+    pre2 = dot(k2f[:, 0:864], im_mid[...])
     total = jnp.zeros((64, 128), F32)
     up = up_ref[...].astype(F32) * 0.125
     for p, (px, pz, py) in enumerate(PHASES):
-        value = pre2[:, p * 128 : (p + 1) * 128] + b2_ref[...]
+        value = pre2[:, p * 128 : (p + 1) * 128] + bias2
         total = total + leaky(value)
         back = (up * slope_of(value)).astype(BF16)
         grad[px, pz, py] = back
         flat_grad[:, p * 128 : (p + 1) * 128] = back
-    grad_bufs = (grad_x, grad_z, grad_d)
+    grad_bufs = sets[2]
     halo_start(2, grad, grad_bufs)
     feat_ref[...] = (total * 0.125).astype(BF16)
 
@@ -280,12 +335,10 @@
     for k in range(1, plane):
         rs_copy(k).start()
 
+    fill(im_grad, grad, grad_bufs, True, True)
     halo_wait(2, grad, grad_bufs)
-    fill(im_grad, grad, grad_bufs, True)
-    back1 = dot(k2b_ref[...], im_grad[...]).astype(BF16)
-    for px in range(2):
-        joined = dot(back1[:, px * 512 : (px + 1) * 512], join_ref[...])
-        pg_ref[:, px * 512 : (px + 1) * 512] = joined.astype(BF16)
+    fill(im_grad, grad, grad_bufs, True, False)
+    rounded = dot(k2b[...], im_grad[...]).astype(BF16)
 
     for k in range(1, plane):
         rs_copy(k).wait()
@@ -296,18 +349,23 @@
     for k in range(1, n_gx):
         gx_copy(0, across, k).start()
 
-    back1 = back1.astype(F32) * 0.125
-    folded = jnp.zeros((32, 128), F32)
+    back1 = rounded.astype(F32) * 0.125
     for p in range(8):
-        grad1 = (back1 * slope_of(pre1[p * 32 : (p + 1) * 32, :])).astype(BF16)
-        full = dot_nt(grad1, patch[...])
-        high = full.astype(BF16)
-        low = (full - high.astype(F32)).astype(BF16)
-        choose = taps_ref[:, p * 256 : (p + 1) * 256]
-        folded = folded + (dot_nt(high, choose) + dot_nt(low, choose))
+        slope = slope_of(pre1[p * 32 : (p + 1) * 32, :])
+        grads1[p * 32 : (p + 1) * 32, :] = (back1 * slope).astype(BF16)
+    full = dot_nt(grads1[...], patch[...])
+    full = jnp.concatenate([full[p * 32 : (p + 1) * 32] for p in range(8)], axis=1)
+    high = full.astype(BF16)
+    low = (full - high.astype(F32)).astype(BF16)
+    folded = dot(jnp.concatenate([high, low], axis=0), taps_t[...])
+    folded = folded[0:32] + folded[32:64]
     one_all[rank] = folded
     for k in range(1, plane):
         plane_copy(1, one_all, k).start()
+
+    for px in range(2):
+        joined = dot(rounded[:, px * 512 : (px + 1) * 512], join[...])
+        pg_ref[:, px * 512 : (px + 1) * 512] = joined.astype(BF16)
 
     scale = 1.0 / n_dp
     for k in range(1, n_gx):
@@ -329,25 +387,24 @@
         gx_copy(1, one_gx, k).start()
     for k in range(1, plane):
         plane_copy(2, gathered, k).wait()
-    two_ref[...] = gathered[...]
+    whole = gathered[...].reshape(64, 896)
+    for j in range(7):
+        end = min(j * 128 + 128, 864)
+        two_ref[j * 128 : end, :] = whole[:, j * 128 : (j + 1) * 128].T[0 : end - j * 128]
     for k in range(1, n_gx):
         gx_copy(1, one_gx, k).wait()
     mine = one_gx[0]
     for j in range(1, n_gx):
         mine = mine + one_gx[j]
-    one_ref[...] = mine * scale
+    mine = (mine * scale).T
+    for t in range(27):
+        one_ref[t] = mine[t * 4 : t * 4 + 4]
 
 
 def local(sizes, volume, kernel_one, bias_one, kernel_two, bias_two, upstream):
     n_dp, n_gx, n_yz = sizes
     plane = n_dp * n_yz
     rows = 64 // plane
-    x = volume.reshape(4, 4, 4, 4, 128)
-    x = jnp.transpose(x, (1, 3, 0, 2, 4)).reshape(64, 512)
-    k1 = jnp.pad(kernel_one.reshape(32, 108), ((0, 0), (0, 20)))
-    k2 = kernel_two.reshape(64, 32, 27)
-    k2f = jnp.transpose(k2, (0, 2, 1)).reshape(64, 864)
-    k2b = jnp.transpose(k2, (1, 2, 0)).reshape(32, 1728)
     vmem = pl.BlockSpec(memory_space=pltpu.VMEM)
 
     def halos(n, more, rows):
@@ -360,10 +417,10 @@
         out_shape=(
             jax.ShapeDtypeStruct((64, 128), BF16),
             jax.ShapeDtypeStruct((32, 1024), BF16),
-            jax.ShapeDtypeStruct((32, 128), F32),
-            jax.ShapeDtypeStruct((plane, rows, 896), F32),
+            jax.ShapeDtypeStruct((27, 4, 32), F32),
+            jax.ShapeDtypeStruct((864, 64), F32),
         ),
-        in_specs=[vmem] * 10,
+        in_specs=[vmem] * 6,
         out_specs=(vmem,) * 4,
         scratch_shapes=[
             *halos(4, (), 16),
@@ -381,6 +438,15 @@
             pltpu.VMEM((plane, rows, 896), F32),
             pltpu.VMEM((plane, 32, 128), F32),
             pltpu.VMEM((n_gx, 32, 128), F32),
+            pltpu.VMEM((64, 512), F32),
+            pltpu.VMEM((128, 128), F32),
+            pltpu.VMEM((64, 896), BF16),
+            pltpu.VMEM((32, 1728), BF16),
+            pltpu.VMEM((512, 512), BF16),
+            pltpu.VMEM((512, 512), BF16),
+            pltpu.VMEM((128, 2048), BF16),
+            pltpu.VMEM((2048, 128), BF16),
+            pltpu.VMEM((256, 1024), BF16),
             pltpu.SemaphoreType.DMA((3, 8)),
             pltpu.SemaphoreType.DMA((3, 8)),
             pltpu.SemaphoreType.DMA((3, plane - 1)),
@@ -395,24 +461,18 @@
             flops=900_000_000, bytes_accessed=3_000_000, transcendentals=0
         ),
     )(
-        x,
+        volume.reshape(4, 4, 2048),
         upstream.reshape(64, 128),
-        k1,
-        jnp.broadcast_to(bias_one[:, None], (32, 128)),
-        k2f,
-        jnp.broadcast_to(bias_two[:, None], (64, 128)),
-        k2b,
-        jnp.asarray(split_matrix(), BF16),
-        jnp.asarray(join_matrix(), BF16),
-        jnp.asarray(tap_matrix(), BF16),
+        jnp.transpose(kernel_one, (2, 3, 4, 1, 0)).reshape(27, 4, 32),
+        bias_one.reshape(1, 32),
+        jnp.transpose(kernel_two, (2, 3, 4, 1, 0)).reshape(864, 64),
+        bias_two.reshape(1, 64),
     )
-    two = two.reshape(64, 896)[:, :864].reshape(64, 27, 32)
-    two = jnp.transpose(two, (0, 2, 1)).reshape(64, 32, 3, 3, 3)
     return (
         feat.reshape(1, 64, 1, 1, 128),
         pg.reshape(1, 32, 2, 1, 512),
-        one[:, :108].reshape(32, 4, 3, 3, 3),
-        two,
+        jnp.transpose(one.reshape(3, 3, 3, 4, 32), (4, 3, 0, 1, 2)),
+        jnp.transpose(two.reshape(3, 3, 3, 32, 64), (4, 3, 0, 1, 2)),
     )
 
 

time: 39 us -> 36.2 us (0.928)
  Pallas kernels: 30.3 us -> 28.7 us
  local copies, waits for them, and re-layouts: 7.72 us -> 6.54 us
    reshape x8 -> x0, local copies, waits for them, and re-layouts: 2.58 us -> none  [the longest x1 1.09 us: local(): k2 = kernel_two.reshape(64, 32, 27)]
    unnamed x19 -> x15, local copies, waits for them, and re-layouts: 4.23 us -> 5.88 us
    pallas_call x1, Pallas kernels: 30.3 us -> 28.7 us  [local(): pl.pallas_call(functools.partial(kernel, sizes), out_shape=(jax.ShapeDtyp...]
where the time goes in v1:
time: 36.2 us; the launch traced here: 35.9 us
  Pallas kernels  28.7 us (79%)
  local copies, waits for them, and re-layouts  6.54 us (18%)
  between operations  0.66 us (2%)
    pallas_call x1, Pallas kernels, local(): pl.pallas_call(functools.partial(kernel, sizes), out_shape=(jax.ShapeDtyp...  28.7 us
    unnamed x15, local copies, waits for them, and re-layouts  5.88 us

profile of v1, /device:TPU:0, one launch (start us, length us, event | category | flops | bytes accessed | tf_op | source)
XLA Modules:
  0.0 35.9 jit_solution(13832407601992622785)
XLA Ops:
  0.6 0.0 copy-start.4
  0.6 0.0 copy-start.5
  0.7 0.6 %copy-done.4 = f32[32]{0:T(128)S(1)} copy-done((f32[32]{0:T(128)S(1)}, f32[32]{0:T(128)}, u32[]{:S(2)}) %copy-start.4) | copy-done | bytes 152
  1.3 0.0 copy-done.5
  1.3 0.0 copy-start
  1.3 0.9 %copy-done = bf16[64,32,3,3,3]{0,1,4,3,2:T(8,128)(2,1)S(1)} copy-done((bf16[64,32,3,3,3]{0,1,4,3,2:T(8,128)(2,1)S(1)}, bf16[64,32,3,3,3]{0,1,4,3,2:T(8,128)(2,1)}, u32[]{:S(2)}) %copy-start) | copy-done | bytes 110616
  2.2 0.0 copy-start.1
  2.2 0.8 %copy-done.1 = bf16[1,4,4,1,2048]{4,2,3,1,0:T(4,128)(2,1)S(1)} copy-done((bf16[1,4,4,1,2048]{4,2,3,1,0:T(4,128)(2,1)S(1)}, bf16[1,4,4,1,2048]{4,2,3,1,0:T(4,128)(2,1)}, u32[]{:S(2)}) %copy-start.1) | copy-done | bytes 65560
  3.1 0.0 copy-start.2
  3.1 0.7 %copy-done.2 = bf16[32,4,3,3,3]{0,1,4,3,2:T(4,128)(2,1)S(1)} copy-done((bf16[32,4,3,3,3]{0,1,4,3,2:T(4,128)(2,1)S(1)}, bf16[32,4,3,3,3]{0,1,4,3,2:T(4,128)(2,1)}, u32[]{:S(2)}) %copy-start.2) | copy-done | bytes 6936
  3.8 0.0 copy-start.3
  3.8 0.7 %copy-done.3 = bf16[1,64,1,1,128]{4,1,3,2,0:T(8,128)(2,1)S(1)} copy-done((bf16[1,64,1,1,128]{4,1,3,2,0:T(8,128)(2,1)S(1)}, bf16[1,64,1,1,128]{4,1,3,2,0:T(8,128)(2,1)}, u32[]{:S(2)}) %copy-start.3) | copy-done | bytes 16408
  4.5 28.7 %shard_map.93 = (bf16[64,128]{1,0:T(8,128)(2,1)S(1)}, bf16[32,1024]{1,0:T(8,128)(2,1)S(1)}, f32[27,4,32]{2,1,0:T(4,128)S(1)}, f32[864,64]{1,0:T(8,128)S(1)}) custom-call(bf16[4,4,2048]{2,1,0:T(4,128)(2,1)S(1)} %bitcast.22, bf16[64,128]{1,0:T(8,128)(2,1)S(1)} %bitcast.24, bf16[27,4,32]{2,1,0:T(4,128)(2,1)S(1)} %bitcast.23, f32[1,32]{1,0:T(1,128)S(1)} %bitcast.25, ...), custom_call_target="tpu_custom_call" | custom-call | flops 900000000 | bytes 3000000 | tf_op jit(solution)/shard_map/pallas_call | solution.py:415
  33.3 0.7 %reshape.45 = bf16[1,32,2,1,512]{4,2,1,3,0:T(2,128)(2,1)} reshape(bf16[32,1024]{1,0:T(8,128)(2,1)S(1)} %get-tuple-element.9) | data formatting | bytes 131072 | tf_op jit(solution)/shard_map/reshape | solution.py:473
  33.9 0.6 %copy.14 = bf16[1,64,1,1,128]{4,1,3,2,0:T(8,128)(2,1)} copy(bf16[1,64,1,1,128]{4,1,3,2,0:T(8,128)(2,1)S(1)} %bitcast.20) | data formatting | bytes 32768
  34.5 0.6 %copy.15 = f32[32,4,3,3,3]{0,1,4,3,2:T(4,128)} copy(f32[32,4,3,3,3]{0,1,4,3,2:T(4,128)S(1)} %bitcast.19) | data formatting | bytes 27648
  35.2 0.8 %copy.16 = f32[64,32,3,3,3]{0,1,4,3,2:T(8,128)} copy(f32[64,32,3,3,3]{0,1,4,3,2:T(8,128)S(1)} %bitcast.18) | data formatting | bytes 442368
Async XLA Ops:
  0.6 0.7 %copy-start.4 = (f32[32]{0:T(128)S(1)}, f32[32]{0:T(128)}, u32[]{:S(2)}) copy-start(f32[32]{0:T(128)} %param.8) | copy-start | bytes 388
  0.6 0.7 %copy-start.5 = (f32[64]{0:T(128)S(1)}, f32[64]{0:T(128)}, u32[]{:S(2)}) copy-start(f32[64]{0:T(128)} %param.10) | copy-start | bytes 772
  1.3 0.9 %copy-start = (bf16[64,32,3,3,3]{0,1,4,3,2:T(8,128)(2,1)S(1)}, bf16[64,32,3,3,3]{0,1,4,3,2:T(8,128)(2,1)}, u32[]{:S(2)}) copy-start(bf16[64,32,3,3,3]{0,1,4,3,2:T(8,128)(2,1)} %param.9) | copy-start | bytes 331780
  2.2 0.8 %copy-start.1 = (bf16[1,4,4,1,2048]{4,2,3,1,0:T(4,128)(2,1)S(1)}, bf16[1,4,4,1,2048]{4,2,3,1,0:T(4,128)(2,1)}, u32[]{:S(2)}) copy-start(bf16[1,4,4,1,2048]{4,2,3,1,0:T(4,128)(2,1)} %param.6) | copy-start | bytes 196612
  3.1 0.7 %copy-start.2 = (bf16[32,4,3,3,3]{0,1,4,3,2:T(4,128)(2,1)S(1)}, bf16[32,4,3,3,3]{0,1,4,3,2:T(4,128)(2,1)}, u32[]{:S(2)}) copy-start(bf16[32,4,3,3,3]{0,1,4,3,2:T(4,128)(2,1)} %param.7) | copy-start | bytes 20740
  3.8 0.7 %copy-start.3 = (bf16[1,64,1,1,128]{4,1,3,2,0:T(8,128)(2,1)S(1)}, bf16[1,64,1,1,128]{4,1,3,2,0:T(8,128)(2,1)}, u32[]{:S(2)}) copy-start(bf16[1,64,1,1,128]{4,1,3,2,0:T(8,128)(2,1)} %param.11) | copy-start | bytes 49156

commit v2 on v1

--- a/solution.py
+++ b/solution.py
@@ -66,15 +66,24 @@
 
 
 def kernel(
-    sizes, v_ref, up_ref, k1_ref, b1_ref, k2_ref, b2_ref,
+    sizes, v_hbm, up_hbm, k1_hbm, b1_hbm, k2_hbm, b2_hbm,
     feat_ref, pg_ref, one_ref, two_ref,
     vol, vol_x, vol_z, vol_d, mid, mid_x, mid_z, mid_d, grad, grad_x, grad_z, grad_d,
     w1, patch, pre1, im_mid, im_grad, flat_grad, part, rs, across, gathered, one_all, one_gx,
     cells, k1, k2f, k2b, split, join, taps, taps_t, grads1,
+    v_ref, up_ref, k1_ref, b1_ref, k2_ref, b2_ref, load_sem,
     halo_send, halo_recv, plane_send, plane_recv, gx_send, gx_recv,
 ):
     n_dp, n_gx, n_yz = sizes
     dp, gx, yz = (lax.axis_index("dp"), lax.axis_index("gx"), lax.axis_index("yz"))
+    sources = (v_hbm, k1_hbm, k2_hbm, b1_hbm, b2_hbm, up_hbm)
+    targets = (v_ref, k1_ref, k2_ref, b1_ref, b2_ref, up_ref)
+    loads = [
+        pltpu.make_async_copy(source, target, load_sem.at[i])
+        for i, (source, target) in enumerate(zip(sources, targets))
+    ]
+    for load in loads:
+        load.start()
     plane = n_dp * n_yz
     rank = dp * n_yz + yz
 
@@ -229,6 +238,7 @@
                     patch[row : row + 16, q * 128 : (q + 1) * 128] = high if qy else low
 
     split[...] = one_hot(split_source(), 512)
+    loads[0].wait()
     for c in range(4):
         values = v_ref[c].astype(F32)
         for y in range(16):
@@ -247,6 +257,8 @@
     halo_start(0, vol, vol_bufs)
 
     fill_patch(True)
+    for load in loads[1:]:
+        load.wait()
     k1[...] = jnp.zeros_like(k1)
     for t in range(27):
         k1[t * 4 : t * 4 + 4, 0:32] = k1_ref[t].astype(F32)
@@ -420,7 +432,7 @@
             jax.ShapeDtypeStruct((27, 4, 32), F32),
             jax.ShapeDtypeStruct((864, 64), F32),
         ),
-        in_specs=[vmem] * 6,
+        in_specs=[pl.BlockSpec(memory_space=pltpu.HBM)] * 6,
         out_specs=(vmem,) * 4,
         scratch_shapes=[
             *halos(4, (), 16),
@@ -447,6 +459,13 @@
             pltpu.VMEM((128, 2048), BF16),
             pltpu.VMEM((2048, 128), BF16),
             pltpu.VMEM((256, 1024), BF16),
+            pltpu.VMEM((4, 4, 2048), BF16),
+            pltpu.VMEM((64, 128), BF16),
+            pltpu.VMEM((27, 4, 32), BF16),
+            pltpu.VMEM((1, 32), F32),
+            pltpu.VMEM((864, 64), BF16),
+            pltpu.VMEM((1, 64), F32),
+            pltpu.SemaphoreType.DMA((6,)),
             pltpu.SemaphoreType.DMA((3, 8)),
             pltpu.SemaphoreType.DMA((3, 8)),
             pltpu.SemaphoreType.DMA((3, plane - 1)),
@@ -455,7 +474,7 @@
             pltpu.SemaphoreType.DMA((2, n_gx - 1)),
         ],
         compiler_params=pltpu.CompilerParams(
-            collective_id=0, has_side_effects=True, vmem_limit_bytes=48 * 2**20
+            collective_id=0, has_side_effects=True, vmem_limit_bytes=64 * 2**20 - 65536
         ),
         cost_estimate=pl.CostEstimate(
             flops=900_000_000, bytes_accessed=3_000_000, transcendentals=0

time: 36.2 us -> 35.1 us (0.970)
  local copies, waits for them, and re-layouts: 6.54 us -> 4.56 us
  Pallas kernels: 28.7 us -> 29.6 us
    unnamed x15 -> x7, local copies, waits for them, and re-layouts: 5.88 us -> 3.04 us
    pallas_call x1, Pallas kernels: 28.7 us -> 29.6 us  [local(): pl.pallas_call(functools.partial(kernel, sizes), out_shape=(jax.ShapeDtyp...]
    reshape x1, local copies, waits for them, and re-layouts: 0.66 us -> 1.52 us  [local(): pg.reshape(1, 32, 2, 1, 512)]
where the time goes in v2:
time: 35.1 us; the launch traced here: 34.9 us
  Pallas kernels  29.6 us (84%)
  local copies, waits for them, and re-layouts  4.56 us (13%)
  between operations  0.66 us (2%)
    pallas_call x1, Pallas kernels, local(): pl.pallas_call(functools.partial(kernel, sizes), out_shape=(jax.ShapeDtyp...  29.6 us
    unnamed x7, local copies, waits for them, and re-layouts  3.04 us
    reshape x1, local copies, waits for them, and re-layouts, local(): pg.reshape(1, 32, 2, 1, 512)  1.52 us

profile of v2, /device:TPU:0, one launch (start us, length us, event | category | flops | bytes accessed | tf_op | source)
XLA Modules:
  0.0 34.9 jit_solution(12199308780598345224)
XLA Ops:
  0.6 29.6 %shard_map.93 = (bf16[64,128]{1,0:T(8,128)(2,1)}, bf16[32,1024]{1,0:T(8,128)(2,1)}, f32[27,4,32]{2,1,0:T(4,128)}, f32[864,64]{1,0:T(8,128)}) custom-call(bf16[4,4,2048]{2,1,0:T(4,128)(2,1)} %bitcast.23, bf16[64,128]{1,0:T(8,128)(2,1)} %bitcast.25, bf16[27,4,32]{2,1,0:T(4,128)(2,1)} %bitcast.24, f32[1,32]{1,0:T(1,128)} %bitcast.26, bf16[864,64]{1,0:T(8,128)(2,1)} %bitcast.22, ...), custom_call_target="tpu_custom_call" | custom-call | flops 900000000 | bytes 3000000 | tf_op jit(solution)/shard_map/pallas_call | solution.py:427
  30.3 0.0 copy-start.1
  30.3 0.0 copy-start
  30.3 1.5 %reshape.45 = bf16[1,32,2,1,512]{4,2,1,3,0:T(2,128)(2,1)} reshape(bf16[32,1024]{1,0:T(8,128)(2,1)} %get-tuple-element.9) | data formatting | bytes 131072 | tf_op jit(solution)/shard_map/reshape | solution.py:492
  31.8 0.0 copy-done.1
  31.8 0.6 %copy.14 = bf16[1,64,1,1,128]{4,1,3,2,0:T(8,128)(2,1)} copy(bf16[1,64,1,1,128]{4,1,3,2,0:T(8,128)(2,1)S(1)} %bitcast.21) | data formatting | bytes 32768
  32.4 0.0 copy-done
  32.4 0.6 %copy.15 = f32[32,4,3,3,3]{0,1,4,3,2:T(4,128)} copy(f32[32,4,3,3,3]{0,1,4,3,2:T(4,128)S(1)} %bitcast.20) | data formatting | bytes 27648
  33.1 1.8 %copy.16 = f32[64,32,3,3,3]{0,1,4,3,2:T(8,128)} copy(f32[64,32,3,3,3]{0,1,4,3,2:T(8,128)} %bitcast.18) | data formatting | bytes 442368
Async XLA Ops:
  30.3 1.5 %copy-start.1 = (bf16[64,128]{1,0:T(8,128)(2,1)S(1)}, bf16[64,128]{1,0:T(8,128)(2,1)}, u32[]{:S(2)}) copy-start(bf16[64,128]{1,0:T(8,128)(2,1)} %get-tuple-element.8) | copy-start | bytes 49156
  30.3 2.1 %copy-start = (f32[27,4,32]{2,1,0:T(4,128)S(1)}, f32[27,4,32]{2,1,0:T(4,128)}, u32[]{:S(2)}) copy-start(f32[27,4,32]{2,1,0:T(4,128)} %get-tuple-element.10) | copy-start | bytes 41476
